TPU v7x, 128 devices: a whole 4x4x4 slice. The times are simulated.
128 devices in a mesh: layer: 4 (over y), grid: 32 (over x, z, core).
Axes of the slice: x: 4, y: 4, z: 4, core: 2. Of those that a mesh axis runs over, the one named last changes fastest.
Arguments:
- leaf_inverse: float32 [4, 32, 4, 128, 128], P('layer', 'grid'), may hold values from -1 to 2
- leaf_coupling: float32 [4, 32, 4, 128, 128], P('layer', 'grid'), may hold values from -0.5 to 0.5
- leaf_rhs: float32 [4, 32, 4, 128, 128], P('layer', 'grid'), may hold values from -6 to 6
- mid_inverse: float32 [4, 32, 2, 128, 128], P('layer', 'grid'), may hold values from -1 to 2
- mid_coupling: float32 [4, 32, 2, 128, 128], P('layer', 'grid'), may hold values from -0.375 to 0.375
- mid_rhs: float32 [4, 32, 2, 128, 128], P('layer', 'grid'), may hold values from -6 to 6
- mid_top: float32 [4, 32, 2, 4096, 128], P('layer', 'grid'), may hold values from -0.0546875 to 0.0546875
- root_inverse: float32 [4, 32, 128, 128], P('layer', 'grid'), may hold values from -1 to 2
- root_top: float32 [4, 32, 4096, 128], P('layer', 'grid'), may hold values from -0.0546875 to 0.0546875
- root_rhs: float32 [4, 32, 128, 128], P('layer', 'grid'), may hold values from -6 to 6
- top_inverse: float32 [32, 128, 128], P('grid'), may hold values from -1 to 2
- top_factor: float32 [32, 128, 4096], P('grid'), may hold values from -0.25 to 0.25
- top_rhs: float32 [32, 128, 128], P('grid'), may hold values from -6 to 6
- top_pattern: int32 [32, 32], P('grid'), may hold values from 0 to 1, as said below
Outputs:
- leaf_solution: float32 [4, 32, 4, 128, 128], P('layer', 'grid')
- mid_solution: float32 [4, 32, 2, 128, 128], P('layer', 'grid')
- root_solution: float32 [4, 32, 128, 128], P('layer', 'grid')
- top_solution: float32 [32, 128, 128], P('grid')
Inputs may be any that keep to these rules, and one draw needn't show every extreme that they name: `top_pattern`: entries (i, j) with j // 4 >= i // 4 are not read; entry (i, 0) is 1 for every i >= 4.
All inputs are finite; a program needn't handle non-finite values.
Results may differ from a plain program's by a relative error of at most 0.00011.
Values sent between devices are 32-bit elements; how exact they have to be, the bound alone decides.
No kernel may reach another device: no remote copies, remote signals or barrier semaphores. Data moves between devices by JAX's collectives and lax.ppermute only.
A program may use at most 64 MiB of HBM per device.

v0:
```python
import jax
import jax.numpy as jnp
from jax import lax
from jax.sharding import PartitionSpec as P

SPAN = 4


def product(spec, left, right):
    return jnp.einsum(
        spec, left, right, precision=lax.Precision.HIGHEST, preferred_element_type=jnp.float32
    )


def transposed(left, right):
    return lax.dot_general(
        left,
        right,
        (((0,), (0,)), ((), ())),
        precision=lax.Precision.HIGHEST,
        preferred_element_type=jnp.float32,
    )


def pack_slot(value, slot, span):
    picks = (jnp.arange(span) == slot)[:, None, None]
    return jnp.where(picks, value[None], jnp.zeros((), jnp.float32))


def local(
    leaf_inverse,
    leaf_coupling,
    leaf_rhs,
    mid_inverse,
    mid_coupling,
    mid_rhs,
    mid_top,
    root_inverse,
    root_top,
    root_rhs,
    top_inverse,
    top_factor,
    top_rhs,
    top_pattern,
):
    block_width = leaf_inverse.shape[-1]
    columns = leaf_rhs.shape[-1]
    blocks_top = lax.axis_size("grid")
    position = lax.axis_index("grid")
    span = SPAN
    group_count = blocks_top // span
    own_group = position // span
    leaf_inv = leaf_inverse[0, 0]
    leaf_links = leaf_coupling[0, 0]
    forward_leaf = product("pab,pbr->par", leaf_inv, leaf_rhs[0, 0])
    pulled = (
        product("pab,pbr->par", leaf_links, forward_leaf)
        .reshape(-1, 2, block_width, columns)
        .sum(axis=1)
    )
    forward_mid = product("mab,mbr->mar", mid_inverse[0, 0], mid_rhs[0, 0] - pulled)
    root_input = root_rhs[0, 0] - product("mab,mbr->ar", mid_coupling[0, 0], forward_mid)
    forward_root = product("ab,br->ar", root_inverse[0, 0], root_input)
    root_panel = root_top[0, 0]
    mid_panel = mid_top[0, 0]
    root_rows = root_panel
    mid_rows = mid_panel
    summed = product("kb,br->kr", root_rows, forward_root) + product(
        "mkb,mbr->kr", mid_rows, forward_mid
    )
    partial_sums = lax.psum_scatter(
        summed.reshape(1 * lax.axis_size("grid"), block_width, columns),
        "grid",
        scatter_dimension=0,
        tiled=True,
    )
    reduced = lax.psum(partial_sums, "layer")
    residual = top_rhs[0] - reduced[0]
    top_inv = top_inverse[0]
    factor_row = top_factor[0]
    pattern_row = top_pattern[0]

    def weights_of(group):
        stored = lax.dynamic_slice_in_dim(pattern_row, group * span, span)
        return jnp.where(group < own_group, stored, 0).astype(jnp.float32)

    def panel_of(group):
        return lax.dynamic_slice_in_dim(
            factor_row, group * span * block_width, span * block_width, 1
        )

    def forward_step(group, carried):
        residual, solved_own = carried
        candidate = jnp.dot(
            top_inv, residual, precision=lax.Precision.HIGHEST, preferred_element_type=jnp.float32
        )
        slot = position - group * span
        solved = lax.psum(pack_slot(candidate, slot, span), "grid")
        scaled = (weights_of(group)[:, None, None] * solved).reshape(span * block_width, columns)
        update = jnp.dot(
            panel_of(group),
            scaled,
            precision=lax.Precision.HIGHEST,
            preferred_element_type=jnp.float32,
        )
        residual = residual - update
        solved_own = jnp.where(own_group == group, candidate, solved_own)
        return (residual, solved_own)

    residual, forward_top = lax.fori_loop(
        0, group_count, forward_step, (residual, jnp.zeros_like(residual))
    )

    def contribution(group, back_own):
        terms = transposed(panel_of(group), back_own).reshape(span, block_width, columns)
        return weights_of(group)[:, None, None] * terms

    def settle(group, pulled_group, back_own):
        slot = jnp.clip(position - group * span, 0, span - 1)
        pulled_top = lax.dynamic_index_in_dim(pulled_group, slot, 0, keepdims=False)
        candidate = transposed(top_inv, forward_top - pulled_top)
        return jnp.where(own_group == group, candidate, back_own)

    def back_step(sweep_step, back_own):
        group = group_count - 1 - sweep_step
        pulled_group = lax.psum(contribution(group, back_own), "grid")
        return settle(group, pulled_group, back_own)

    back_own = lax.fori_loop(0, group_count, back_step, jnp.zeros_like(forward_top))
    shard_piece = lax.all_gather(back_own[None], "grid", axis=0, tiled=True)
    amount = shard_piece.shape[0]
    flat_rows = shard_piece.reshape(amount * block_width, columns)
    root_rows = root_panel
    mid_rows = mid_panel
    root_pull = transposed(root_rows, flat_rows)
    mid_pull = product("mkb,kr->mbr", mid_rows, flat_rows)
    back_root = product("ba,br->ar", root_inverse[0, 0], forward_root - root_pull)
    back_mid = product(
        "mba,mbr->mar",
        mid_inverse[0, 0],
        forward_mid - product("mab,ar->mbr", mid_coupling[0, 0], back_root) - mid_pull,
    )
    parent = jnp.repeat(back_mid, 2, axis=0)
    back_leaf = product(
        "pba,pbr->par", leaf_inv, forward_leaf - product("pab,par->pbr", leaf_links, parent)
    )
    return (back_leaf[None, None], back_mid[None, None], back_root[None, None], back_own[None])


def solution(mesh):
    placed = (
        P("layer", "grid", None, None, None),
        P("layer", "grid", None, None, None),
        P("layer", "grid", None, None, None),
        P("layer", "grid", None, None, None),
        P("layer", "grid", None, None, None),
        P("layer", "grid", None, None, None),
        P("layer", "grid", None, None, None),
        P("layer", "grid", None, None),
        P("layer", "grid", None, None),
        P("layer", "grid", None, None),
        P("grid", None, None),
        P("grid", None, None),
        P("grid", None, None),
        P("grid", None),
    )
    return jax.shard_map(
        local,
        mesh=mesh,
        in_specs=placed,
        out_specs=(
            P("layer", "grid", None, None, None),
            P("layer", "grid", None, None, None),
            P("layer", "grid", None, None),
            P("grid", None, None),
        ),
        check_vma=False,
    )
```

profile of v0, /device:TPU:1, one launch (start us, length us, event | category | flops | bytes accessed | tf_op | source)
XLA Modules:
  0.0 1938.6 jit_solution(1425876203916425412)
XLA Ops:
  12.7 6.5 convolution_bitcast_fusion.1
  26.2 80.7 %reduce-scatter.2.cloned.1.call-done = f32[1,128,128]{2,1,0:T(8,128)} async-done(((f32[32,128,128]{2,1,0:T(8,128)}), f32[1,128,128]{2,1,0:T(8,128)}) %reduce-scatter.2.cloned.1.call-update) | async-done | bytes 65552 | tf_op jit(solution)/shard_map/reduce_scatter | solution.py:71
  106.9 41.9 %all-reduce.4.cloned.1.call-done = f32[1,128,128]{2,1,0:T(8,128)} async-done(((f32[1,128,128]{2,1,0:T(8,128)}), f32[1,128,128]{2,1,0:T(8,128)}) %all-reduce.4.cloned.1.call-update) | async-done | bytes 65552 | tf_op jit(solution)/shard_map/psum | solution.py:77
  149.7 868.9 %while.34 = (s32[]{:T(128)}, f32[128,128]{1,0:T(8,128)S(1)}, f32[128,128]{1,0:T(8,128)S(1)}, f32[128,4096]{1,0:T(8,128)}, s32[]{:T(128)}, /*index=5*/s32[32]{0:T...) while((s32[]{:T(128)}, f32[128,128]{1,0:T(8,128)S(1)}, ...), condition=%wide.region_5.6_spmd.clone, body=%wide.region_3.5_spmd.clone.sunk | while | flops 126074896 | bytes 3408247 | solution.py:110
  150.9 107.7 %all-reduce.6.cloned.1.call-done = f32[4,128,128]{2,1,0:T(8,128)} async-done(((f32[4,128,128]{2,1,0:T(8,128)}), f32[4,128,128]{2,1,0:T(8,128)}) %all-reduce.6.cloned.1.call-update) | async-done | bytes 262160 | tf_op jit(solution)/shard_map/while/body/eval_jaxpr/psum | solution.py:98
  262.2 104.5 %all-reduce.6.cloned.1.call-done = f32[4,128,128]{2,1,0:T(8,128)} async-done(((f32[4,128,128]{2,1,0:T(8,128)}), f32[4,128,128]{2,1,0:T(8,128)}) %all-reduce.6.cloned.1.call-update) | async-done | bytes 262160 | tf_op jit(solution)/shard_map/while/body/eval_jaxpr/psum | solution.py:98
  370.3 104.5 %all-reduce.6.cloned.1.call-done = f32[4,128,128]{2,1,0:T(8,128)} async-done(((f32[4,128,128]{2,1,0:T(8,128)}), f32[4,128,128]{2,1,0:T(8,128)}) %all-reduce.6.cloned.1.call-update) | async-done | bytes 262160 | tf_op jit(solution)/shard_map/while/body/eval_jaxpr/psum | solution.py:98
  478.4 104.5 %all-reduce.6.cloned.1.call-done = f32[4,128,128]{2,1,0:T(8,128)} async-done(((f32[4,128,128]{2,1,0:T(8,128)}), f32[4,128,128]{2,1,0:T(8,128)}) %all-reduce.6.cloned.1.call-update) | async-done | bytes 262160 | tf_op jit(solution)/shard_map/while/body/eval_jaxpr/psum | solution.py:98
  586.5 104.8 %all-reduce.6.cloned.1.call-done = f32[4,128,128]{2,1,0:T(8,128)} async-done(((f32[4,128,128]{2,1,0:T(8,128)}), f32[4,128,128]{2,1,0:T(8,128)}) %all-reduce.6.cloned.1.call-update) | async-done | bytes 262160 | tf_op jit(solution)/shard_map/while/body/eval_jaxpr/psum | solution.py:98
  694.9 104.8 %all-reduce.6.cloned.1.call-done = f32[4,128,128]{2,1,0:T(8,128)} async-done(((f32[4,128,128]{2,1,0:T(8,128)}), f32[4,128,128]{2,1,0:T(8,128)}) %all-reduce.6.cloned.1.call-update) | async-done | bytes 262160 | tf_op jit(solution)/shard_map/while/body/eval_jaxpr/psum | solution.py:98
  803.3 104.8 %all-reduce.6.cloned.1.call-done = f32[4,128,128]{2,1,0:T(8,128)} async-done(((f32[4,128,128]{2,1,0:T(8,128)}), f32[4,128,128]{2,1,0:T(8,128)}) %all-reduce.6.cloned.1.call-update) | async-done | bytes 262160 | tf_op jit(solution)/shard_map/while/body/eval_jaxpr/psum | solution.py:98
  911.7 104.5 %all-reduce.6.cloned.1.call-done = f32[4,128,128]{2,1,0:T(8,128)} async-done(((f32[4,128,128]{2,1,0:T(8,128)}), f32[4,128,128]{2,1,0:T(8,128)}) %all-reduce.6.cloned.1.call-update) | async-done | bytes 262160 | tf_op jit(solution)/shard_map/while/body/eval_jaxpr/psum | solution.py:98
  1018.6 852.6 %while.35 = (s32[]{:T(128)}, f32[128,128]{0,1:T(8,128)S(1)}, s32[]{:T(128)}, s32[32]{0:T(128)S(1)}, f32[128,4096]{1,0:T(8,128)}, /*index=5*/s32[]{:T(128)}, f32[...) while((s32[]{:T(128)}, f32[128,128]{0,1:T(8,128)S(1)}, ...), condition=%wide.region_8.9_spmd.clone, body=%wide.region_6.8_spmd.clone.sunk | while | flops 126025744 | bytes 3015076 | solution.py:129
  1021.2 103.1 %all-reduce.8.cloned.1.call-done = f32[4,128,128]{2,1,0:T(8,128)} async-done(((f32[4,128,128]{2,1,0:T(8,128)}), f32[4,128,128]{2,1,0:T(8,128)}) %all-reduce.8.cloned.1.call-update) | async-done | bytes 262160 | tf_op jit(solution)/shard_map/while/body/eval_jaxpr/psum | solution.py:126
  1128.0 102.8 %all-reduce.8.cloned.1.call-done = f32[4,128,128]{2,1,0:T(8,128)} async-done(((f32[4,128,128]{2,1,0:T(8,128)}), f32[4,128,128]{2,1,0:T(8,128)}) %all-reduce.8.cloned.1.call-update) | async-done | bytes 262160 | tf_op jit(solution)/shard_map/while/body/eval_jaxpr/psum | solution.py:126
  1234.5 103.1 %all-reduce.8.cloned.1.call-done = f32[4,128,128]{2,1,0:T(8,128)} async-done(((f32[4,128,128]{2,1,0:T(8,128)}), f32[4,128,128]{2,1,0:T(8,128)}) %all-reduce.8.cloned.1.call-update) | async-done | bytes 262160 | tf_op jit(solution)/shard_map/while/body/eval_jaxpr/psum | solution.py:126
  1341.3 102.8 %all-reduce.8.cloned.1.call-done = f32[4,128,128]{2,1,0:T(8,128)} async-done(((f32[4,128,128]{2,1,0:T(8,128)}), f32[4,128,128]{2,1,0:T(8,128)}) %all-reduce.8.cloned.1.call-update) | async-done | bytes 262160 | tf_op jit(solution)/shard_map/while/body/eval_jaxpr/psum | solution.py:126
  1447.8 102.8 %all-reduce.8.cloned.1.call-done = f32[4,128,128]{2,1,0:T(8,128)} async-done(((f32[4,128,128]{2,1,0:T(8,128)}), f32[4,128,128]{2,1,0:T(8,128)}) %all-reduce.8.cloned.1.call-update) | async-done | bytes 262160 | tf_op jit(solution)/shard_map/while/body/eval_jaxpr/psum | solution.py:126
  1554.3 102.8 %all-reduce.8.cloned.1.call-done = f32[4,128,128]{2,1,0:T(8,128)} async-done(((f32[4,128,128]{2,1,0:T(8,128)}), f32[4,128,128]{2,1,0:T(8,128)}) %all-reduce.8.cloned.1.call-update) | async-done | bytes 262160 | tf_op jit(solution)/shard_map/while/body/eval_jaxpr/psum | solution.py:126
  1660.8 102.8 %all-reduce.8.cloned.1.call-done = f32[4,128,128]{2,1,0:T(8,128)} async-done(((f32[4,128,128]{2,1,0:T(8,128)}), f32[4,128,128]{2,1,0:T(8,128)}) %all-reduce.8.cloned.1.call-update) | async-done | bytes 262160 | tf_op jit(solution)/shard_map/while/body/eval_jaxpr/psum | solution.py:126
  1767.3 102.8 %all-reduce.8.cloned.1.call-done = f32[4,128,128]{2,1,0:T(8,128)} async-done(((f32[4,128,128]{2,1,0:T(8,128)}), f32[4,128,128]{2,1,0:T(8,128)}) %all-reduce.8.cloned.1.call-update) | async-done | bytes 262160 | tf_op jit(solution)/shard_map/while/body/eval_jaxpr/psum | solution.py:126
  1873.6 46.3 %all-gather.3.cloned.1.call-done = f32[4096,128]{0,1:T(8,128)} async-done(((f32[128,128]{0,1:T(8,128)}), f32[4096,128]{0,1:T(8,128)}) %all-gather.3.cloned.1.call-update) | async-done | bytes 2097168 | tf_op jit(solution)/shard_map/all_gather | solution.py:130
  1919.9 3.9 fusion.34
  1924.3 3.8 fusion.28
  (164 shorter events, 77.0 us)
Async XLA Ops:
  7.2 12.7 copy-start
  7.2 99.7 %reduce-scatter.2.cloned.1.call-start = ((), (), s32[]{:S(2)}) async-start(), calls=%async_computation.1 | async-start | bytes 2162688 | tf_op jit(solution)/shard_map/reduce_scatter | solution.py:71
  12.7 6.8 copy-start.8
  26.1 122.7 %copy-start.9 = (f32[1,128,128]{2,1,0:T(8,128)S(1)}, f32[1,128,128]{2,1,0:T(8,128)}, u32[]{:S(2)}) copy-start(f32[1,128,128]{2,1,0:T(8,128)} %param.30) | copy-start | bytes 196612
  26.1 123.6 %copy-start.3 = (f32[1,128,128]{2,1,0:T(8,128)S(1)}, f32[1,128,128]{2,1,0:T(8,128)}, u32[]{:S(2)}) copy-start(f32[1,128,128]{2,1,0:T(8,128)} %param.28) | copy-start | bytes 196612
  26.1 123.6 %copy-start.11 = (s32[1,32]{1,0:T(1,128)S(1)}, s32[1,32]{1,0:T(1,128)}, u32[]{:S(2)}) copy-start(s32[1,32]{1,0:T(1,128)} %param.31) | copy-start | bytes 388
  26.2 122.7 %all-reduce.4.cloned.1.call-start = ((), (), s32[]{:S(2)}) async-start(), calls=%async_computation.2 | async-start | bytes 131072 | tf_op jit(solution)/shard_map/psum | solution.py:77
  149.7 108.9 %all-reduce.6.cloned.1.call-start = ((), (), s32[]{:S(2)}) async-start(), calls=%async_computation.4 | async-start | bytes 524288 | tf_op jit(solution)/shard_map/while/body/eval_jaxpr/psum | solution.py:98
  261.0 105.7 %all-reduce.6.cloned.1.call-start = ((), (), s32[]{:S(2)}) async-start(), calls=%async_computation.4 | async-start | bytes 524288 | tf_op jit(solution)/shard_map/while/body/eval_jaxpr/psum | solution.py:98
  369.1 105.7 %all-reduce.6.cloned.1.call-start = ((), (), s32[]{:S(2)}) async-start(), calls=%async_computation.4 | async-start | bytes 524288 | tf_op jit(solution)/shard_map/while/body/eval_jaxpr/psum | solution.py:98
  477.2 105.7 %all-reduce.6.cloned.1.call-start = ((), (), s32[]{:S(2)}) async-start(), calls=%async_computation.4 | async-start | bytes 524288 | tf_op jit(solution)/shard_map/while/body/eval_jaxpr/psum | solution.py:98
  585.3 106.0 %all-reduce.6.cloned.1.call-start = ((), (), s32[]{:S(2)}) async-start(), calls=%async_computation.4 | async-start | bytes 524288 | tf_op jit(solution)/shard_map/while/body/eval_jaxpr/psum | solution.py:98
  693.7 106.0 %all-reduce.6.cloned.1.call-start = ((), (), s32[]{:S(2)}) async-start(), calls=%async_computation.4 | async-start | bytes 524288 | tf_op jit(solution)/shard_map/while/body/eval_jaxpr/psum | solution.py:98
  802.1 106.0 %all-reduce.6.cloned.1.call-start = ((), (), s32[]{:S(2)}) async-start(), calls=%async_computation.4 | async-start | bytes 524288 | tf_op jit(solution)/shard_map/while/body/eval_jaxpr/psum | solution.py:98
  910.5 105.7 %all-reduce.6.cloned.1.call-start = ((), (), s32[]{:S(2)}) async-start(), calls=%async_computation.4 | async-start | bytes 524288 | tf_op jit(solution)/shard_map/while/body/eval_jaxpr/psum | solution.py:98
  1018.6 105.7 %all-reduce.8.cloned.1.call-start = ((), (), s32[]{:S(2)}) async-start(), calls=%async_computation.5 | async-start | bytes 524288 | tf_op jit(solution)/shard_map/while/body/eval_jaxpr/psum | solution.py:126
  1125.5 105.4 %all-reduce.8.cloned.1.call-start = ((), (), s32[]{:S(2)}) async-start(), calls=%async_computation.5 | async-start | bytes 524288 | tf_op jit(solution)/shard_map/while/body/eval_jaxpr/psum | solution.py:126
  1232.0 105.7 %all-reduce.8.cloned.1.call-start = ((), (), s32[]{:S(2)}) async-start(), calls=%async_computation.5 | async-start | bytes 524288 | tf_op jit(solution)/shard_map/while/body/eval_jaxpr/psum | solution.py:126
  1338.8 105.3 %all-reduce.8.cloned.1.call-start = ((), (), s32[]{:S(2)}) async-start(), calls=%async_computation.5 | async-start | bytes 524288 | tf_op jit(solution)/shard_map/while/body/eval_jaxpr/psum | solution.py:126
  1445.3 105.4 %all-reduce.8.cloned.1.call-start = ((), (), s32[]{:S(2)}) async-start(), calls=%async_computation.5 | async-start | bytes 524288 | tf_op jit(solution)/shard_map/while/body/eval_jaxpr/psum | solution.py:126
  1551.8 105.3 %all-reduce.8.cloned.1.call-start = ((), (), s32[]{:S(2)}) async-start(), calls=%async_computation.5 | async-start | bytes 524288 | tf_op jit(solution)/shard_map/while/body/eval_jaxpr/psum | solution.py:126
  1658.3 105.4 %all-reduce.8.cloned.1.call-start = ((), (), s32[]{:S(2)}) async-start(), calls=%async_computation.5 | async-start | bytes 524288 | tf_op jit(solution)/shard_map/while/body/eval_jaxpr/psum | solution.py:126
  1764.8 105.3 %all-reduce.8.cloned.1.call-start = ((), (), s32[]{:S(2)}) async-start(), calls=%async_computation.5 | async-start | bytes 524288 | tf_op jit(solution)/shard_map/while/body/eval_jaxpr/psum | solution.py:126
  1871.3 48.7 %all-gather.3.cloned.1.call-start = ((), (), s32[]{:S(2)}) async-start(), calls=%async_computation.3 | async-start | bytes 2162688 | tf_op jit(solution)/shard_map/all_gather | solution.py:130
  (7 other events, 27.2 us)
Sparse Core Ops, SparseCore 0:
  26.3 80.5 reduce-scatter.1
  109.2 39.6 all-reduce.3
  154.7 103.8 all-reduce.5
  265.7 100.9 all-reduce.5
  373.8 100.9 all-reduce.5
  481.9 100.9 all-reduce.5
  590.3 100.9 all-reduce.5
  698.7 100.9 all-reduce.5
  807.1 100.9 all-reduce.5
  915.2 100.9 all-reduce.5
  1023.3 100.9 all-reduce.7
  1129.8 100.9 all-reduce.7
  1236.6 100.9 all-reduce.7
  1343.1 100.9 all-reduce.7
  1449.6 100.9 all-reduce.7
  1556.1 100.9 all-reduce.7
  1662.6 100.9 all-reduce.7
  1769.1 100.9 all-reduce.7
  1875.1 44.7 all-gather.2
where the time goes:
time: 1940 us
  waiting for transfers between devices  1830 us (94%)
  matrix products  58.2 us (3%)
  other arithmetic  23.1 us (1%)
    psum x8, waiting for transfers between devices, forward_step(): solved = lax.psum(pack_slot(candidate, slot, span), 'grid')  840 us
    psum x8, waiting for transfers between devices, back_step(): pulled_group = lax.psum(contribution(group, back_own), 'grid')  823 us
    reduce_scatter x1, waiting for transfers between devices, local(): lax.psum_scatter(summed.reshape(1 * lax.axis_size('grid'), block_width, c...  80.7 us
    all_gather x1, waiting for transfers between devices, local(): shard_piece = lax.all_gather(back_own[None], 'grid', axis=0, tiled=True)  46.3 us
    psum x1, waiting for transfers between devices, local(): reduced = lax.psum(partial_sums, 'layer')  41.9 us
  transfers between devices with their start and end apart: 19, of which 19 were waited for; matrix products, arithmetic and copies ran while one was open for 0% of the time, Pallas kernels for 0%

commit v1 on v0

--- a/solution.py
+++ b/solution.py
@@ -74,7 +74,11 @@
         scatter_dimension=0,
         tiled=True,
     )
-    reduced = lax.psum(partial_sums, "layer")
+    size = lax.axis_size("layer")
+    reduced, reach = (partial_sums, 1)
+    while reach < size:
+        reduced = reduced + lax.ppermute(reduced, "layer", [(i, i ^ reach) for i in range(size)])
+        reach = 2 * reach
     residual = top_rhs[0] - reduced[0]
     top_inv = top_inverse[0]
     factor_row = top_factor[0]

time: 1940 us -> 1910 us (0.985)
  waiting for transfers between devices: 1830 us -> 1800 us
    psum x1 -> x0, waiting for transfers between devices: 41.9 us -> none  [local(): reduced = lax.psum(partial_sums, 'layer')]
  transfers between devices with their start and end apart: 19 -> 20, of which waited for: 19 -> 20; matrix products, arithmetic and copies ran while one was open for 0% -> 0% of each run, Pallas kernels for 0% -> 0%
where the time goes in v1:
time: 1910 us
  waiting for transfers between devices  1800 us (94%)
  matrix products  58.2 us (3%)
  other arithmetic  23.1 us (1%)
    psum x8, waiting for transfers between devices, forward_step(): solved = lax.psum(pack_slot(candidate, slot, span), 'grid')  839 us
    psum x8, waiting for transfers between devices, back_step(): pulled_group = lax.psum(contribution(group, back_own), 'grid')  826 us
    reduce_scatter x1, waiting for transfers between devices, local(): lax.psum_scatter(summed.reshape(1 * lax.axis_size('grid'), block_width, c...  80.7 us
    all_gather x1, waiting for transfers between devices, local(): shard_piece = lax.all_gather(back_own[None], 'grid', axis=0, tiled=True)  45.9 us
  transfers between devices with their start and end apart: 20, of which 20 were waited for; matrix products, arithmetic and copies ran while one was open for 0% of the time, Pallas kernels for 0%

profile of v1, /device:TPU:1, one launch (start us, length us, event | category | flops | bytes accessed | tf_op | source)
XLA Modules:
  0.0 1906.0 jit_solution(17261903448020268999)
XLA Ops:
  12.7 6.5 convolution_bitcast_fusion.1
  19.8 3.4 fusion.14
  26.2 80.7 %reduce-scatter.2.cloned.1.call-done = f32[1,128,128]{2,1,0:T(8,128)} async-done(((f32[32,128,128]{2,1,0:T(8,128)}), f32[1,128,128]{2,1,0:T(8,128)}) %reduce-scatter.2.cloned.1.call-update) | async-done | bytes 65552 | tf_op jit(solution)/shard_map/reduce_scatter | solution.py:71
  115.9 867.7 %while.34 = (s32[]{:T(128)}, f32[128,128]{1,0:T(8,128)S(1)}, f32[128,128]{1,0:T(8,128)S(1)}, f32[128,4096]{1,0:T(8,128)}, s32[]{:T(128)}, /*index=5*/s32[32]{0:T...) while((s32[]{:T(128)}, f32[128,128]{1,0:T(8,128)S(1)}, ...), condition=%wide.region_4.5_spmd.clone, body=%wide.region_2.4_spmd.clone.sunk | while | flops 126074896 | bytes 3408247 | solution.py:114
  117.1 108.5 %all-reduce.3.cloned.1.call-done = f32[4,128,128]{2,1,0:T(8,128)} async-done(((f32[4,128,128]{2,1,0:T(8,128)}), f32[4,128,128]{2,1,0:T(8,128)}) %all-reduce.3.cloned.1.call-update) | async-done | bytes 262160 | tf_op jit(solution)/shard_map/while/body/eval_jaxpr/psum | solution.py:102
  229.2 104.5 %all-reduce.3.cloned.1.call-done = f32[4,128,128]{2,1,0:T(8,128)} async-done(((f32[4,128,128]{2,1,0:T(8,128)}), f32[4,128,128]{2,1,0:T(8,128)}) %all-reduce.3.cloned.1.call-update) | async-done | bytes 262160 | tf_op jit(solution)/shard_map/while/body/eval_jaxpr/psum | solution.py:102
  337.3 104.1 %all-reduce.3.cloned.1.call-done = f32[4,128,128]{2,1,0:T(8,128)} async-done(((f32[4,128,128]{2,1,0:T(8,128)}), f32[4,128,128]{2,1,0:T(8,128)}) %all-reduce.3.cloned.1.call-update) | async-done | bytes 262160 | tf_op jit(solution)/shard_map/while/body/eval_jaxpr/psum | solution.py:102
  445.0 104.1 %all-reduce.3.cloned.1.call-done = f32[4,128,128]{2,1,0:T(8,128)} async-done(((f32[4,128,128]{2,1,0:T(8,128)}), f32[4,128,128]{2,1,0:T(8,128)}) %all-reduce.3.cloned.1.call-update) | async-done | bytes 262160 | tf_op jit(solution)/shard_map/while/body/eval_jaxpr/psum | solution.py:102
  552.8 104.1 %all-reduce.3.cloned.1.call-done = f32[4,128,128]{2,1,0:T(8,128)} async-done(((f32[4,128,128]{2,1,0:T(8,128)}), f32[4,128,128]{2,1,0:T(8,128)}) %all-reduce.3.cloned.1.call-update) | async-done | bytes 262160 | tf_op jit(solution)/shard_map/while/body/eval_jaxpr/psum | solution.py:102
  660.6 104.5 %all-reduce.3.cloned.1.call-done = f32[4,128,128]{2,1,0:T(8,128)} async-done(((f32[4,128,128]{2,1,0:T(8,128)}), f32[4,128,128]{2,1,0:T(8,128)}) %all-reduce.3.cloned.1.call-update) | async-done | bytes 262160 | tf_op jit(solution)/shard_map/while/body/eval_jaxpr/psum | solution.py:102
  768.7 104.5 %all-reduce.3.cloned.1.call-done = f32[4,128,128]{2,1,0:T(8,128)} async-done(((f32[4,128,128]{2,1,0:T(8,128)}), f32[4,128,128]{2,1,0:T(8,128)}) %all-reduce.3.cloned.1.call-update) | async-done | bytes 262160 | tf_op jit(solution)/shard_map/while/body/eval_jaxpr/psum | solution.py:102
  876.7 104.5 %all-reduce.3.cloned.1.call-done = f32[4,128,128]{2,1,0:T(8,128)} async-done(((f32[4,128,128]{2,1,0:T(8,128)}), f32[4,128,128]{2,1,0:T(8,128)}) %all-reduce.3.cloned.1.call-update) | async-done | bytes 262160 | tf_op jit(solution)/shard_map/while/body/eval_jaxpr/psum | solution.py:102
  983.6 855.3 %while.35 = (s32[]{:T(128)}, f32[128,128]{0,1:T(8,128)S(1)}, s32[]{:T(128)}, s32[32]{0:T(128)S(1)}, f32[128,4096]{1,0:T(8,128)}, /*index=5*/s32[]{:T(128)}, f32[...) while((s32[]{:T(128)}, f32[128,128]{0,1:T(8,128)S(1)}, ...), condition=%wide.region_7.8_spmd.clone, body=%wide.region_5.7_spmd.clone.sunk | while | flops 126025744 | bytes 3015076 | solution.py:133
  986.1 103.2 %all-reduce.5.cloned.1.call-done = f32[4,128,128]{2,1,0:T(8,128)} async-done(((f32[4,128,128]{2,1,0:T(8,128)}), f32[4,128,128]{2,1,0:T(8,128)}) %all-reduce.5.cloned.1.call-update) | async-done | bytes 262160 | tf_op jit(solution)/shard_map/while/body/eval_jaxpr/psum | solution.py:130
  1093.0 103.5 %all-reduce.5.cloned.1.call-done = f32[4,128,128]{2,1,0:T(8,128)} async-done(((f32[4,128,128]{2,1,0:T(8,128)}), f32[4,128,128]{2,1,0:T(8,128)}) %all-reduce.5.cloned.1.call-update) | async-done | bytes 262160 | tf_op jit(solution)/shard_map/while/body/eval_jaxpr/psum | solution.py:130
  1200.1 103.2 %all-reduce.5.cloned.1.call-done = f32[4,128,128]{2,1,0:T(8,128)} async-done(((f32[4,128,128]{2,1,0:T(8,128)}), f32[4,128,128]{2,1,0:T(8,128)}) %all-reduce.5.cloned.1.call-update) | async-done | bytes 262160 | tf_op jit(solution)/shard_map/while/body/eval_jaxpr/psum | solution.py:130
  1306.9 103.5 %all-reduce.5.cloned.1.call-done = f32[4,128,128]{2,1,0:T(8,128)} async-done(((f32[4,128,128]{2,1,0:T(8,128)}), f32[4,128,128]{2,1,0:T(8,128)}) %all-reduce.5.cloned.1.call-update) | async-done | bytes 262160 | tf_op jit(solution)/shard_map/while/body/eval_jaxpr/psum | solution.py:130
  1414.1 103.2 %all-reduce.5.cloned.1.call-done = f32[4,128,128]{2,1,0:T(8,128)} async-done(((f32[4,128,128]{2,1,0:T(8,128)}), f32[4,128,128]{2,1,0:T(8,128)}) %all-reduce.5.cloned.1.call-update) | async-done | bytes 262160 | tf_op jit(solution)/shard_map/while/body/eval_jaxpr/psum | solution.py:130
  1520.9 103.2 %all-reduce.5.cloned.1.call-done = f32[4,128,128]{2,1,0:T(8,128)} async-done(((f32[4,128,128]{2,1,0:T(8,128)}), f32[4,128,128]{2,1,0:T(8,128)}) %all-reduce.5.cloned.1.call-update) | async-done | bytes 262160 | tf_op jit(solution)/shard_map/while/body/eval_jaxpr/psum | solution.py:130
  1627.7 103.2 %all-reduce.5.cloned.1.call-done = f32[4,128,128]{2,1,0:T(8,128)} async-done(((f32[4,128,128]{2,1,0:T(8,128)}), f32[4,128,128]{2,1,0:T(8,128)}) %all-reduce.5.cloned.1.call-update) | async-done | bytes 262160 | tf_op jit(solution)/shard_map/while/body/eval_jaxpr/psum | solution.py:130
  1734.6 103.2 %all-reduce.5.cloned.1.call-done = f32[4,128,128]{2,1,0:T(8,128)} async-done(((f32[4,128,128]{2,1,0:T(8,128)}), f32[4,128,128]{2,1,0:T(8,128)}) %all-reduce.5.cloned.1.call-update) | async-done | bytes 262160 | tf_op jit(solution)/shard_map/while/body/eval_jaxpr/psum | solution.py:130
  1841.1 45.9 %all-gather.3.cloned.1.call-done = f32[4096,128]{0,1:T(8,128)} async-done(((f32[128,128]{0,1:T(8,128)}), f32[4096,128]{0,1:T(8,128)}) %all-gather.3.cloned.1.call-update) | async-done | bytes 2097168 | tf_op jit(solution)/shard_map/all_gather | solution.py:134
  1887.0 3.9 fusion.34
  1891.4 3.8 fusion.28
  (166 shorter events, 81.5 us)
Async XLA Ops:
  7.2 12.7 copy-start
  7.2 99.7 %reduce-scatter.2.cloned.1.call-start = ((), (), s32[]{:S(2)}) async-start(), calls=%async_computation.1 | async-start | bytes 2162688 | tf_op jit(solution)/shard_map/reduce_scatter | solution.py:71
  26.1 89.7 %copy-start.10 = (f32[1,128,128]{2,1,0:T(8,128)S(1)}, f32[1,128,128]{2,1,0:T(8,128)}, u32[]{:S(2)}) copy-start(f32[1,128,128]{2,1,0:T(8,128)} %param.30) | copy-start | bytes 196612
  26.1 89.7 %copy-start.3 = (f32[1,128,128]{2,1,0:T(8,128)S(1)}, f32[1,128,128]{2,1,0:T(8,128)}, u32[]{:S(2)}) copy-start(f32[1,128,128]{2,1,0:T(8,128)} %param.28) | copy-start | bytes 196612
  26.1 89.7 %copy-start.11 = (s32[1,32]{1,0:T(1,128)S(1)}, s32[1,32]{1,0:T(1,128)}, u32[]{:S(2)}) copy-start(s32[1,32]{1,0:T(1,128)} %param.31) | copy-start | bytes 388
  106.9 3.3 collective-permute-start
  111.1 4.8 collective-permute-start.1
  115.9 109.7 %all-reduce.3.cloned.1.call-start = ((), (), s32[]{:S(2)}) async-start(), calls=%async_computation.3 | async-start | bytes 524288 | tf_op jit(solution)/shard_map/while/body/eval_jaxpr/psum | solution.py:102
  228.0 105.7 %all-reduce.3.cloned.1.call-start = ((), (), s32[]{:S(2)}) async-start(), calls=%async_computation.3 | async-start | bytes 524288 | tf_op jit(solution)/shard_map/while/body/eval_jaxpr/psum | solution.py:102
  336.1 105.3 %all-reduce.3.cloned.1.call-start = ((), (), s32[]{:S(2)}) async-start(), calls=%async_computation.3 | async-start | bytes 524288 | tf_op jit(solution)/shard_map/while/body/eval_jaxpr/psum | solution.py:102
  443.8 105.4 %all-reduce.3.cloned.1.call-start = ((), (), s32[]{:S(2)}) async-start(), calls=%async_computation.3 | async-start | bytes 524288 | tf_op jit(solution)/shard_map/while/body/eval_jaxpr/psum | solution.py:102
  551.6 105.3 %all-reduce.3.cloned.1.call-start = ((), (), s32[]{:S(2)}) async-start(), calls=%async_computation.3 | async-start | bytes 524288 | tf_op jit(solution)/shard_map/while/body/eval_jaxpr/psum | solution.py:102
  659.4 105.7 %all-reduce.3.cloned.1.call-start = ((), (), s32[]{:S(2)}) async-start(), calls=%async_computation.3 | async-start | bytes 524288 | tf_op jit(solution)/shard_map/while/body/eval_jaxpr/psum | solution.py:102
  767.5 105.7 %all-reduce.3.cloned.1.call-start = ((), (), s32[]{:S(2)}) async-start(), calls=%async_computation.3 | async-start | bytes 524288 | tf_op jit(solution)/shard_map/while/body/eval_jaxpr/psum | solution.py:102
  875.5 105.7 %all-reduce.3.cloned.1.call-start = ((), (), s32[]{:S(2)}) async-start(), calls=%async_computation.3 | async-start | bytes 524288 | tf_op jit(solution)/shard_map/while/body/eval_jaxpr/psum | solution.py:102
  983.6 105.7 %all-reduce.5.cloned.1.call-start = ((), (), s32[]{:S(2)}) async-start(), calls=%async_computation.4 | async-start | bytes 524288 | tf_op jit(solution)/shard_map/while/body/eval_jaxpr/psum | solution.py:130
  1090.5 106.0 %all-reduce.5.cloned.1.call-start = ((), (), s32[]{:S(2)}) async-start(), calls=%async_computation.4 | async-start | bytes 524288 | tf_op jit(solution)/shard_map/while/body/eval_jaxpr/psum | solution.py:130
  1197.6 105.7 %all-reduce.5.cloned.1.call-start = ((), (), s32[]{:S(2)}) async-start(), calls=%async_computation.4 | async-start | bytes 524288 | tf_op jit(solution)/shard_map/while/body/eval_jaxpr/psum | solution.py:130
  1304.4 106.0 %all-reduce.5.cloned.1.call-start = ((), (), s32[]{:S(2)}) async-start(), calls=%async_computation.4 | async-start | bytes 524288 | tf_op jit(solution)/shard_map/while/body/eval_jaxpr/psum | solution.py:130
  1411.6 105.7 %all-reduce.5.cloned.1.call-start = ((), (), s32[]{:S(2)}) async-start(), calls=%async_computation.4 | async-start | bytes 524288 | tf_op jit(solution)/shard_map/while/body/eval_jaxpr/psum | solution.py:130
  1518.4 105.7 %all-reduce.5.cloned.1.call-start = ((), (), s32[]{:S(2)}) async-start(), calls=%async_computation.4 | async-start | bytes 524288 | tf_op jit(solution)/shard_map/while/body/eval_jaxpr/psum | solution.py:130
  1625.2 105.7 %all-reduce.5.cloned.1.call-start = ((), (), s32[]{:S(2)}) async-start(), calls=%async_computation.4 | async-start | bytes 524288 | tf_op jit(solution)/shard_map/while/body/eval_jaxpr/psum | solution.py:130
  1732.1 105.7 %all-reduce.5.cloned.1.call-start = ((), (), s32[]{:S(2)}) async-start(), calls=%async_computation.4 | async-start | bytes 524288 | tf_op jit(solution)/shard_map/while/body/eval_jaxpr/psum | solution.py:130
  1838.9 48.1 %all-gather.3.cloned.1.call-start = ((), (), s32[]{:S(2)}) async-start(), calls=%async_computation.2 | async-start | bytes 2162688 | tf_op jit(solution)/shard_map/all_gather | solution.py:134
  (8 other events, 34.0 us)
Sparse Core Ops, SparseCore 0:
  26.3 80.5 reduce-scatter.1
  120.5 105.0 all-reduce.2
  232.6 100.9 all-reduce.2
  340.4 100.9 all-reduce.2
  448.2 100.9 all-reduce.2
  555.9 100.9 all-reduce.2
  664.0 100.9 all-reduce.2
  772.1 100.9 all-reduce.2
  880.2 100.9 all-reduce.2
  988.3 100.9 all-reduce.4
  1095.4 100.9 all-reduce.4
  1202.2 100.9 all-reduce.4
  1309.4 100.9 all-reduce.4
  1416.2 100.9 all-reduce.4
  1523.1 100.9 all-reduce.4
  1629.9 100.9 all-reduce.4
  1736.7 100.9 all-reduce.4
  1842.2 44.7 all-gather.2
